TPU v7x, 32 devices: a whole 2x2x4 slice. The times are simulated.
32 devices in a mesh: groups: 2 (over x), dp: 8 (over z, y), tensor: 2 (over core).
Axes of the slice: x: 2, y: 2, z: 4, core: 2. Of those that a mesh axis runs over, the one named last changes fastest.
Arguments:
- output_gradient: bfloat16 [2048, 4096], P(('groups', 'dp'), 'tensor'), parts along dimension 0, may hold values from -6 to 6
- gate_preactivation: bfloat16 [2048, 14336], P(('groups', 'tensor'), 'dp'), parts along dimension 0, may hold values from -6 to 6
- up_preactivation: bfloat16 [2048, 14336], P(('groups', 'tensor'), 'dp'), parts along dimension 0, may hold values from -6 to 6
- frozen_down_weight: bfloat16 [14336, 4096], P('dp', 'tensor'), may hold values from -0.046875 to 0.046875
- adapter_input_factor: bfloat16 [16, 14336, 128], P('groups', 'dp'), parts along dimension 0, may hold values from -0.14941406 to 0.14941406
- adapter_output_factor: bfloat16 [16, 128, 4096], P(('groups', 'dp'), None, 'tensor'), parts along dimension 0, may hold values from -0.14941406 to 0.14941406
- tenant_token_count: int32 [16], P('groups'), parts along dimension 0, may hold values from 1 to 512, 1024 in all
- tenant_owner_index: int32 [16], P('groups'), parts along dimension 0, may hold values from 0 to 7, each once
- token_expert_index: int32 [2048, 2], P('groups'), parts along dimension 0, may hold values from 0 to 7, all different within a row
- routing_weight_pair: float32 [2048, 2], P('groups'), parts along dimension 0, may hold values from 0.2 to 1
Outputs:
- d_gate: bfloat16 [2048, 14336], P(('groups', 'tensor'), 'dp'), parts along dimension 0
- d_up: bfloat16 [2048, 14336], P(('groups', 'tensor'), 'dp'), parts along dimension 0
- grad_a: float32 [16, 14336, 128], P(('groups', 'tensor'), 'dp'), parts along dimension 0
- grad_b: float32 [16, 128, 4096], P(('groups', 'dp'), None, 'tensor'), parts along dimension 0
There are 2 independent parts, one for each index of `groups`. A program takes and returns all parts, laid end to end along the dimension named above; an argument that names none is the same for every part. Nothing has to cross between parts.
Inputs may be any that keep to these rules, and one draw needn't show every extreme that they name: `tenant_token_count`: tenant i holds the tokens from the sum of the counts before it onward; the counts sum to 1024 and the largest is exactly 512. `tenant_owner_index`: each owner index owns exactly one tenant. `token_expert_index`: the two experts of a token differ.
All inputs are finite; a program needn't handle non-finite values.
Results may differ from a plain program's by a relative error of at most 0.001.
Values may be sent and summed in bfloat16 or wider, within the bound.
A program may use at most 128 MiB of HBM per device.

v0:
```python
import jax
import jax.numpy as jnp
from jax import lax
from jax.sharding import PartitionSpec as P

EXPERT_RANK = 16


adapter_scale = 2.0


def tables(
    tenant_token_count, tenant_owner_index, token_expert_index, routing_weight_pair, column_span
):
    tokens = token_expert_index.shape[0]
    tenants = tenant_token_count.shape[0]
    ends = jnp.cumsum(tenant_token_count)
    positions = lax.broadcasted_iota(jnp.int32, (tokens, 1), 0)
    token_tenant = jnp.sum((positions >= ends[None, :]).astype(jnp.int32), axis=1)
    tenant_ids = lax.broadcasted_iota(jnp.int32, (1, tenants), 1)
    tenant_hot = (token_tenant[:, None] == tenant_ids).astype(jnp.int32)
    token_slot = jnp.sum(tenant_hot * tenant_owner_index[None, :], axis=1)
    expert_col = lax.broadcasted_iota(jnp.int32, (1, column_span), 1) // EXPERT_RANK
    mix = routing_weight_pair[:, 0:1] * (token_expert_index[:, 0:1] == expert_col).astype(
        jnp.float32
    )
    mix = mix + routing_weight_pair[:, 1:2] * (token_expert_index[:, 1:2] == expert_col).astype(
        jnp.float32
    )
    return (ends, token_slot, mix)


def segment_sizes(ends, counts, lower_row, upper_row):
    starts = ends - counts
    return jnp.clip(ends, lower_row, upper_row) - jnp.clip(starts, lower_row, upper_row)


def tenant_outer(rows_left, rows_right, sizes):
    numbers = lax.RaggedDotDimensionNumbers(
        dot_dimension_numbers=(((0,), (0,)), ((), ())),
        lhs_ragged_dimensions=[0],
        rhs_group_dimensions=[],
    )
    return lax.ragged_dot_general(
        rows_left,
        rows_right,
        sizes,
        numbers,
        precision=lax.Precision.HIGHEST,
        preferred_element_type=jnp.float32,
    )


def shards(
    output_gradient,
    gate_preactivation,
    up_preactivation,
    frozen_down_weight,
    adapter_input_factor,
    adapter_output_factor,
    tenant_token_count,
    tenant_owner_index,
    token_expert_index,
    routing_weight_pair,
):
    highest = lax.Precision.HIGHEST
    tokens = token_expert_index.shape[0]
    half_rows = gate_preactivation.shape[0]
    column_span = adapter_input_factor.shape[2]
    hidden_cols = frozen_down_weight.shape[0]
    owner_index = lax.axis_index("dp")
    half_start = lax.axis_index("tensor") * half_rows
    ends, token_slot, mix = tables(
        tenant_token_count, tenant_owner_index, token_expert_index, routing_weight_pair, column_span
    )
    own_rows = (token_slot == owner_index).astype(jnp.float32)[:, None]
    half_length_list = segment_sizes(ends, tenant_token_count, half_start, half_start + half_rows)
    half_mix = lax.dynamic_slice_in_dim(mix, half_start, half_rows, 0)
    gate = gate_preactivation.astype(jnp.float32)
    up = up_preactivation.astype(jnp.float32)
    sig = jax.nn.sigmoid(gate)
    silu = gate * sig
    hidden_state = silu * up
    input_factor_wide = adapter_input_factor.astype(jnp.float32)
    latent_partial = lax.ragged_dot(
        hidden_state,
        input_factor_wide,
        half_length_list,
        precision=highest,
        preferred_element_type=jnp.float32,
    )
    padded = jnp.zeros((tokens, column_span), jnp.float32)
    padded = lax.dynamic_update_slice_in_dim(padded, latent_partial, half_start, 0)
    z_all = lax.psum(padded, ("dp", "tensor"))
    r_rows = adapter_scale * z_all * mix * own_rows
    stacked_weight = jnp.concatenate([frozen_down_weight, adapter_output_factor[0]], axis=0)
    piece = lax.all_gather(output_gradient, "dp", axis=0, tiled=True)
    product = lax.dot_general(
        piece, stacked_weight, (((1,), (1,)), ((), ())), preferred_element_type=jnp.float32
    )
    grad_acc = lax.dot_general(
        r_rows,
        piece.astype(jnp.float32),
        (((0,), (0,)), ((), ())),
        precision=highest,
        preferred_element_type=jnp.float32,
    )
    dense_part = product[:, :hidden_cols]
    q_part = product[:, hidden_cols:] * own_rows
    q_all = lax.psum(q_part, ("dp", "tensor"))
    q_half = lax.dynamic_slice_in_dim(q_all, half_start, half_rows, 0)
    dense_half = lax.psum_scatter(dense_part, "tensor", scatter_dimension=0, tiled=True)
    p_half = adapter_scale * q_half * half_mix
    input_factor_turned = jnp.swapaxes(input_factor_wide, 1, 2)
    grad_hidden = dense_half + lax.ragged_dot(
        p_half,
        input_factor_turned,
        half_length_list,
        precision=highest,
        preferred_element_type=jnp.float32,
    )
    d_up = (grad_hidden * silu).astype(jnp.bfloat16)
    d_gate = (grad_hidden * up * sig * (1.0 + gate * (1.0 - sig))).astype(jnp.bfloat16)
    grad_a_part = tenant_outer(hidden_state, p_half, half_length_list)
    grad_a = lax.psum_scatter(grad_a_part, "tensor", scatter_dimension=0, tiled=True)
    return (d_gate, d_up, grad_a, grad_acc[None])


def solution(mesh):
    in_specs = (
        P(("groups", "dp"), "tensor"),
        P(("groups", "tensor"), "dp"),
        P(("groups", "tensor"), "dp"),
        P("dp", "tensor"),
        P("groups", "dp", None),
        P(("groups", "dp"), None, "tensor"),
        P("groups"),
        P("groups"),
        P("groups", None),
        P("groups", None),
    )
    out_specs = (
        P(("groups", "tensor"), "dp"),
        P(("groups", "tensor"), "dp"),
        P(("groups", "tensor"), "dp", None),
        P(("groups", "dp"), None, "tensor"),
    )
    return jax.shard_map(shards, mesh=mesh, in_specs=in_specs, out_specs=out_specs, check_vma=False)
```

profile of v0, /device:TPU:1, one launch (start us, length us, event | category | flops | bytes accessed | tf_op | source)
XLA Modules:
  0.0 256.8 jit_solution(4019170522131467347)
XLA Ops:
  7.2 0.0 all-gather.2.cloned.1.call-start
  7.2 0.7 all-gather.2.cloned.1.call-update
  7.9 0.0 all-reduce.3.cloned.1.call-start
  8.0 0.8 reduce-window.8
  8.8 1.2 minimum_subtract_fusion
  10.0 1.5 ragged-dot-metadata.1
  11.5 5.0 %convert_multiply_fusion.2 = f32[512,1792]{1,0:T(8,128)} fusion(bf16[512,1792]{1,0:T(8,128)(2,1)} %param.12, bf16[512,1792]{1,0:T(8,128)(2,1)} %param.11), kind=kLoop, calls=%fused_computation.7 | loop fusion | flops 6422528 | bytes 7340032 | tf_op jit(solution)/shard_map/mul | solution.py:83
  16.5 6.8 %convert_bitcast_fusion = (f32[8,128,1792]{1,2,0:T(8,128)}, f32[8,1792,128]{2,1,0:T(8,128)}) fusion(bf16[8,1792,128]{2,1,0:T(8,128)(2,1)S(1)} %copy-done.2), kind=kLoop, calls=%fused_computation.19 | loop fusion | flops 1835008 | bytes 18350080 | tf_op jit(solution)/shard_map/transpose | solution.py:114
  23.3 12.6 %ragged-dot-none = f32[512,128]{1,0:T(8,128)} custom-call(s32[1]{0:T(128)} %get-tuple-element.12, s32[9]{0:T(128)} %get-tuple-element.13, s32[9]{0:T(128)} %get-tuple-element.14, s32[9]{0:T(128)} %get-tuple-element.15, s32[1]{0:T(128)} %get-tuple-element.12, f32[512,1792]{1,0:T(8,128)} %convert_multiply_fusion.2, f32[8,1792,128]{2,1,0:T(8,128)} %get-tuple-element.21), custom_call_target="tpu_custom_call" | custom-call | flops 234881024 | bytes 11272224 | tf_op jit(solution)/shard_map/ragged_dot_general/ragged-dot-none
  35.9 0.1 convert_reduce_fusion
  36.0 0.1 select_reduce_fusion
  36.1 1.0 constant_dynamic-update-slice_fusion
  37.1 0.0 copy-start.3
  37.2 47.3 %all-gather.2.cloned.1.call-done = bf16[1024,2048]{1,0:T(8,128)(2,1)} async-done(((bf16[128,2048]{1,0:T(8,128)(2,1)}), bf16[1024,2048]{1,0:T(8,128)(2,1)}) %all-gather.2.cloned.1.call-update) | async-done | bytes 4194320 | tf_op jit(solution)/shard_map/all_gather | solution.py:97
  84.5 13.2 %fusion.4 = f32[1024,1920]{1,0:T(8,128)S(1)} fusion(bf16[1024,2048]{1,0:T(8,128)(2,1)} %all-gather.2.cloned.1.call-done, bf16[128,2048]{1,0:T(8,128)(2,1)S(1)} %bitcast.26, bf16[1792,2048]{1,0:T(8,128)(2,1)} %param.13), kind=kOutput, calls=%fused_computation.9 | convolution fusion | flops 8068792320 | bytes 19922944 | tf_op jit(solution)/shard_map/dot_general | solution.py:98
  97.7 3.2 %copy-done = f32[1024,1920]{1,0:T(8,128)} copy-done((f32[1024,1920]{1,0:T(8,128)}, f32[1024,1920]{1,0:T(8,128)S(1)}, u32[]{:S(2)}) %copy-start) | copy-done | bytes 7864344
  100.9 1.0 slice_multiply_fusion
  101.9 0.0 all-reduce.3.cloned.1.call-update
  101.9 0.0 reduce-scatter.3.cloned.1.call-start
  101.9 6.6 %slice.24 = f32[1024,1792]{1,0:T(8,128)} slice(f32[1024,1920]{1,0:T(8,128)} %copy-done), slice={[0:1024], [0:1792]} | slice | bytes 14680064 | tf_op jit(solution)/shard_map/slice | solution.py:108
  108.5 0.0 reduce-scatter.3.cloned.1.call-update
  108.5 0.0 reduce-scatter.5.cloned.1.call-start
  108.6 1.5 ragged-dot-metadata
  110.1 0.6 select_add_fusion
  110.8 83.3 %all-reduce.3.cloned.1.call-done = (f32[1024,128]{1,0:T(8,128)}, f32[1024,128]{1,0:T(8,128)}) async-done(((f32[1024,128]{1,0:T(8,128)}, f32[1024,128]{1,0:T(8,128)}), (f32[1024,128]{1,0:T(8,128)}, f32[1024,128]{1,0:T(8,128)})) %all-reduce.3.cloned.1.call-update) | async-done | bytes 1048592 | tf_op jit(solution)/shard_map/psum | solution.py:110
  194.1 1.7 dynamic-slice_multiply_fusion
  195.8 21.3 %ragged-dot-none.1 = f32[8,1792,128]{2,1,0:T(8,128)} custom-call(s32[1]{0:T(128)} %get-tuple-element.8, s32[9]{0:T(128)} %get-tuple-element.9, s32[9]{0:T(128)} %get-tuple-element.10, s32[9]{0:T(128)} %get-tuple-element.11, s32[1]{0:T(128)} %get-tuple-element.8, f32[512,1792]{1,0:T(8,128)} %convert_multiply_fusion.2, f32[512,128]{1,0:T(8,128)} %dynamic-slice_multiply_fusion), custom_call_target="tpu_custom_call" | custom-call | flops 234881024 | bytes 11272224 | tf_op jit(solution)/shard_map/ragged_dot_general/ragged-dot-none
  217.1 0.0 reduce-scatter.5.cloned.1.call-update
  217.1 8.5 %copy.17 = f32[8,128,1792]{2,1,0:T(8,128)} copy(f32[8,128,1792]{1,2,0:T(8,128)} %get-tuple-element.20) | data formatting | bytes 14680064 | tf_op jit(solution)/shard_map/transpose | solution.py:114
  225.7 12.9 %ragged-dot-none.2 = f32[512,1792]{1,0:T(8,128)} custom-call(s32[1]{0:T(128)} %get-tuple-element.12, s32[9]{0:T(128)} %get-tuple-element.13, s32[9]{0:T(128)} %get-tuple-element.14, s32[9]{0:T(128)} %get-tuple-element.15, s32[1]{0:T(128)} %get-tuple-element.12, f32[512,128]{1,0:T(8,128)} %dynamic-slice_multiply_fusion, f32[8,128,1792]{2,1,0:T(8,128)} %copy.17), custom_call_target="tpu_custom_call" | custom-call | flops 234881024 | bytes 11272224 | tf_op jit(solution)/shard_map/ragged_dot_general/ragged-dot-none
  238.6 5.8 %convolution_bitcast_fusion = f32[1,128,2048]{2,1,0:T(8,128)} fusion(bf16[1024,2048]{1,0:T(8,128)(2,1)} %all-gather.2.cloned.1.call-done, f32[1024,128]{1,0:T(8,128)S(1)} %copy-done.4, f32[1024]{0:T(1024)S(1)} %compare_convert_fusion, f32[1024]{0:T(1024)S(1)} %bitcast.19, f32[1024]{0:T(1024)S(1)} %bitcast.17, s32[128]{0:T(128)S(1)} %and_select_fusion, ...), kind=kOutput, calls=%fused_computation.18 | convolution fusion | flops 3222274048 | bytes 5788160 | tf_op jit(solution)/shard_map/dot_general | solution.py:101
  244.4 5.8 %multiply_convert_fusion = (bf16[512,1792]{1,0:T(8,128)(2,1)}, bf16[512,1792]{1,0:T(8,128)(2,1)}) fusion(f32[512,1792]{1,0:T(8,128)} %reduce-scatter.3.cloned.1.call-done, f32[512,1792]{1,0:T(8,128)} %ragged-dot-none.2, bf16[512,1792]{1,0:T(8,128)(2,1)} %param.11, bf16[512,1792]{1,0:T(8,128)(2,1)S(1)} %copy-done.1), kind=kLoop, calls=%fused_computation.17 | loop fusion | flops 14680064 | bytes 14680064 | tf_op jit(solution)/shard_map/convert_element_type | solution.py:122
  (23 shorter events, 0.1 us)
Async XLA Ops:
  7.2 77.3 %all-gather.2.cloned.1.call-start = ((), (), s32[]{:S(2)}) async-start(), calls=%async_computation.2 | async-start | bytes 4718592 | tf_op jit(solution)/shard_map/all_gather | solution.py:97
  7.9 186.2 %all-reduce.3.cloned.1.call-start = ((), (), s32[]{:S(2)}) async-start(), calls=%async_computation.5 | async-start | bytes 2097152 | tf_op jit(solution)/shard_map/psum | solution.py:110
  11.5 5.0 %copy-start.2 = (bf16[8,1792,128]{2,1,0:T(8,128)(2,1)S(1)}, bf16[8,1792,128]{2,1,0:T(8,128)(2,1)}, u32[]{:S(2)}) copy-start(bf16[8,1792,128]{2,1,0:T(8,128)(2,1)} %param.14) | copy-start | bytes 11010052
  23.3 12.7 %copy-start.7 = (s32[8]{0:T(128)S(1)}, s32[8]{0:T(128)}, u32[]{:S(2)}) copy-start(s32[8]{0:T(128)} %param.17) | copy-start | bytes 100
  23.3 61.2 %copy-start.8 = (bf16[1,128,2048]{2,1,0:T(8,128)(2,1)S(1)}, bf16[1,128,2048]{2,1,0:T(8,128)(2,1)}, u32[]{:S(2)}) copy-start(bf16[1,128,2048]{2,1,0:T(8,128)(2,1)} %param.15) | copy-start | bytes 1572868
  37.1 60.6 %copy-start.3 = (f32[1024,128]{1,0:T(8,128)}, f32[1024,128]{1,0:T(8,128)S(1)}, u32[]{:S(2)}) copy-start(f32[1024,128]{1,0:T(8,128)S(1)} %constant_dynamic-update-slice_fusion) | copy-start | bytes 1572868
  97.7 3.2 %copy-start = (f32[1024,1920]{1,0:T(8,128)}, f32[1024,1920]{1,0:T(8,128)S(1)}, u32[]{:S(2)}) copy-start(f32[1024,1920]{1,0:T(8,128)S(1)} %fusion.4) | copy-start | bytes 23592964
  101.9 142.5 %reduce-scatter.3.cloned.1.call-start = ((), (), s32[]{:S(2)}) async-start(), calls=%async_computation.3 | async-start | bytes 11010048 | tf_op jit(solution)/shard_map/reduce_scatter | solution.py:112
  108.5 1.6 copy-start.5
  108.5 1.6 copy-start.6
  108.5 141.7 %reduce-scatter.5.cloned.1.call-start = ((), (), s32[]{:S(2)}) async-start(), calls=%async_computation.4 | async-start | bytes 11010048 | tf_op jit(solution)/shard_map/reduce_scatter | solution.py:125
  225.7 12.9 %copy-start.4 = (f32[1024,128]{1,0:T(8,128)S(1)}, f32[1024,128]{1,0:T(8,128)}, u32[]{:S(2)}) copy-start(f32[1024,128]{1,0:T(8,128)} %get-tuple-element.17) | copy-start | bytes 1572868
  238.6 5.8 %copy-start.1 = (bf16[512,1792]{1,0:T(8,128)(2,1)S(1)}, bf16[512,1792]{1,0:T(8,128)(2,1)}, u32[]{:S(2)}) copy-start(bf16[512,1792]{1,0:T(8,128)(2,1)} %param.12) | copy-start | bytes 5505028
Sparse Core Ops, SparseCore 0:
  10.1 74.2 all-gather.1
  102.0 92.0 all-reduce.2
  196.4 16.1 reduce-scatter.2
  217.3 15.5 reduce-scatter.4
where the time goes:
time: 262 us; the launch traced here: 257 us
  waiting for transfers between devices  131 us (50%)
  Pallas kernels  49.9 us (19%)
  other arithmetic  23.1 us (9%)
  local copies, waits for them, and re-layouts  19.3 us (7%)
  matrix products  19 us (7%)
  between operations  13.9 us (5%)
    psum x1, waiting for transfers between devices, shards(): q_all = lax.psum(q_part, ('dp', 'tensor'))  83.3 us
    all_gather x1, waiting for transfers between devices, shards(): piece = lax.all_gather(output_gradient, 'dp', axis=0, tiled=True)  47.3 us
    another operation x3, Pallas kernels  46.9 us
    dot_general x1, matrix products, shards(): lax.dot_general(piece, stacked_weight, (((1,), (1,)), ((), ())), preferre...  13.2 us
    transpose x1, local copies, waits for them, and re-layouts, shards(): input_factor_turned = jnp.swapaxes(input_factor_wide, 1, 2)  8.54 us
    transpose x1, other arithmetic, shards(): input_factor_turned = jnp.swapaxes(input_factor_wide, 1, 2)  6.82 us
    slice x1, local copies, waits for them, and re-layouts, shards(): dense_part = product[:, :hidden_cols]  6.56 us
    convert_element_type x1, other arithmetic, shards(): d_up = (grad_hidden * silu).astype(jnp.bfloat16)  5.82 us
  transfers between devices with their start and end apart: 4, of which 2 were waited for; matrix products, arithmetic and copies ran while one was open for 17% of the time, Pallas kernels for 19%

commit v1 on v0

v1 whole, which is shorter than its diff:
```python
import functools

import jax
import jax.numpy as jnp
from jax import lax
from jax.experimental import pallas as pl
from jax.experimental.pallas import tpu as pltpu
from jax.sharding import PartitionSpec as P

EXPERT_RANK = 16
ADAPTER_SCALE = 2.0
F32 = jnp.float32
BF16 = jnp.bfloat16
NT = (((1,), (1,)), ((), ()))
TN = (((0,), (0,)), ((), ()))


def split_bf16(x):
    high = x.astype(BF16)
    return high, (x - high.astype(F32)).astype(BF16)


def gather_kernel(
    n, counts, owners, og, gate, up, weight, a_in, b_out, mix,
    dense_out, hid_out, q_out, grad_b_out,
    og_all, w_v, gate_v, up_v, a_v, b_v, hid, prod,
    z_part, z_got, z_all, q_part, q_peer, q_half, q_got, q_all, r_rows,
    load_sem, ring_send, ring_recv, prod_send, prod_recv,
    z_send, z_recv, q_send, q_recv, core_send, core_recv, out_sem,
):
    me = lax.axis_index("dp")
    core = lax.axis_index("tensor")
    other = 1 - core
    half_n = n // 2
    block = og.shape[0]
    sub = block // 2
    tokens = block * n
    rows = tokens // 2
    part = rows // n
    hidden = weight.shape[0]
    tenants = a_in.shape[0]
    span = a_in.shape[2]
    tile = 256 if hidden % 256 == 0 else 128

    def at_ring(position):
        position = lax.rem(position + 2 * n, n)
        return jnp.where(position < half_n, 2 * position, 2 * (n - 1 - position) + 1)

    position = jnp.where(lax.rem(me, 2) == 0, me // 2, n - 1 - me // 2)
    right, left = at_ring(position + 1), at_ring(position - 1)

    loads = []

    def load(source, target):
        copy = pltpu.make_async_copy(source, target, load_sem.at[len(loads)])
        copy.start()
        loads.append(copy)
        return copy

    gate_load = load(gate, gate_v)
    up_load = load(up, up_v)
    a_load = load(a_in, a_v)
    og_load = load(og, og_all.at[pl.ds(0, block)])
    w_load = load(weight, w_v)
    b_load = load(b_out, b_v)

    barrier = pltpu.get_barrier_semaphore()
    for step in range(1, n):
        pl.semaphore_signal(
            barrier, inc=1, device_id={"dp": lax.rem(me + step, n)},
            device_id_type=pl.DeviceIdType.MESH,
        )
    pl.semaphore_signal(
        barrier, inc=1, device_id={"tensor": other}, device_id_type=pl.DeviceIdType.MESH
    )
    pl.semaphore_wait(barrier, n)

    def slot(way, distance):
        if distance == 0:
            return 0
        if distance == half_n:
            return n - 1
        return 1 + 2 * (distance - 1) + way

    def origin(k):
        if k == 0:
            return me
        if k == n - 1:
            return at_ring(position + half_n)
        distance = (k - 1) // 2 + 1
        return at_ring(position - distance) if (k - 1) % 2 == 0 else at_ring(position + distance)

    def hop(way, distance, piece):
        if distance == 1:
            source = og.at[pl.ds(piece * sub, sub)]
        else:
            source = og_all.at[pl.ds(slot(way, distance - 1) * block + piece * sub, sub)]
        return pltpu.make_async_remote_copy(
            src_ref=source,
            dst_ref=og_all.at[pl.ds(slot(way, distance) * block + piece * sub, sub)],
            send_sem=ring_send.at[way, distance - 1, piece],
            recv_sem=ring_recv.at[way, distance - 1, piece],
            device_id={"dp": right if way == 0 else left},
            device_id_type=pl.DeviceIdType.MESH,
        )

    def piece_of(way, order):
        return order if way == 0 else 1 - order

    hops = {}

    def start_hop(way, distance, order):
        piece = piece_of(way, order)
        hops[way, distance, order] = hop(way, distance, piece)
        hops[way, distance, order].start()

    for order in range(2):
        for way in range(2):
            start_hop(way, 1, order)

    def forward(distance, order):
        for way in range(2):
            hops[way, distance, order].wait_recv()
            if distance + 1 < half_n or (distance + 1 == half_n and order == 0):
                start_hop(way, distance + 1, order)

    gate_load.wait()
    up_load.wait()
    height = 16

    def hidden_step(i, carry):
        at = pl.ds(pl.multiple_of(i * height, height), height)
        low_at = pl.ds(pl.multiple_of(rows + i * height, height), height)
        g = gate_v[at, :].astype(F32)
        high, low = split_bf16(g * jax.nn.sigmoid(g) * up_v[at, :].astype(F32))
        hid[at, :] = high
        hid[low_at, :] = low
        return carry

    lax.fori_loop(0, rows // height, hidden_step, 0)

    to_core = {"tensor": other}
    mine = pl.ds(core * rows, rows)
    theirs = pl.ds(other * rows, rows)
    hid_copies = []
    for term in range(2):
        source = hid.at[pl.ds(term * rows, rows)]
        remote = pltpu.make_async_remote_copy(
            src_ref=source, dst_ref=hid_out.at[term, mine],
            send_sem=core_send.at[term], recv_sem=core_recv.at[term],
            device_id=to_core, device_id_type=pl.DeviceIdType.MESH,
        )
        local = pltpu.make_async_copy(source, hid_out.at[term, mine], out_sem.at[term])
        remote.start()
        local.start()
        hid_copies.append((remote, local))

    first = core * rows

    def z_work(lower, upper):
        def body(i, start):
            end = start + counts[i]
            both = jnp.dot(hid[...], a_v[i], preferred_element_type=F32)
            at = lax.broadcasted_iota(jnp.int32, (rows, span), 0) + first
            inside = jnp.logical_and(at >= start, at < end)
            z_part[...] += jnp.where(inside, both[:rows] + both[rows:], 0.0)
            return end

        start = jnp.int32(0)
        for i in range(lower):
            start = start + counts[i]
        lax.fori_loop(lower, upper, body, start)

    def scatter(source, got, send, recv):
        copies = []
        for step in range(1, n):
            to = lax.rem(me + step, n)
            copy = pltpu.make_async_remote_copy(
                src_ref=source.at[pl.ds(pl.multiple_of(to * part, part), part)],
                dst_ref=got.at[step],
                send_sem=send.at[0, step], recv_sem=recv.at[0, step],
                device_id={"dp": to}, device_id_type=pl.DeviceIdType.MESH,
            )
            copy.start()
            copies.append(copy)
        return copies

    def spread(source, got, full, copies, send, recv):
        total = source[pl.ds(pl.multiple_of(me * part, part), part), :]
        for step in range(1, n):
            copies[step - 1].wait_recv()
            total = total + got[step]
        at = pl.ds(pl.multiple_of(first + me * part, part), part)
        full[at, :] = total
        out = []
        for step in range(1, n):
            to = lax.rem(me + step, n)
            copy = pltpu.make_async_remote_copy(
                src_ref=full.at[at], dst_ref=full.at[at],
                send_sem=send.at[1, step], recv_sem=recv.at[1, step],
                device_id={"dp": to}, device_id_type=pl.DeviceIdType.MESH,
            )
            copy.start()
            out.append(copy)
        return out

    def landed(full, recv, send):
        for step in range(1, n):
            source = lax.rem(me + n - step, n)
            at = pl.ds(pl.multiple_of(first + source * part, part), part)
            pltpu.make_async_remote_copy(
                src_ref=full.at[at], dst_ref=full.at[at],
                send_sem=send.at[1, step], recv_sem=recv.at[1, step],
                device_id={"dp": source}, device_id_type=pl.DeviceIdType.MESH,
            ).wait_recv()

    def swap_landed(full, index):
        pltpu.make_async_remote_copy(
            src_ref=full.at[theirs], dst_ref=full.at[theirs],
            send_sem=core_send.at[index], recv_sem=core_recv.at[index],
            device_id=to_core, device_id_type=pl.DeviceIdType.MESH,
        ).wait_recv()

    def swap(full, index):
        copy = pltpu.make_async_remote_copy(
            src_ref=full.at[mine], dst_ref=full.at[mine],
            send_sem=core_send.at[index], recv_sem=core_recv.at[index],
            device_id=to_core, device_id_type=pl.DeviceIdType.MESH,
        )
        copy.start()
        return copy

    own_start, own_end, running = jnp.int32(0), jnp.int32(0), jnp.int32(0)
    for i in range(tenants):
        hit = (owners[i] == me).astype(jnp.int32)
        own_start = own_start + hit * running
        running = running + counts[i]
        own_end = own_end + hit * running

    def own_mask(start, length):
        at = lax.broadcasted_iota(jnp.int32, (length, span), 0) + start
        return jnp.logical_and(at >= own_start, at < own_end)

    def product_copy(k):
        j = origin(k)
        local = lax.rem(j, half_n)
        rows_at = pl.ds(pl.multiple_of(local * block, block), block)
        source = prod.at[pl.ds(k * block, block)]
        return (
            j // half_n,
            pltpu.make_async_remote_copy(
                src_ref=source, dst_ref=dense_out.at[1, rows_at],
                send_sem=prod_send.at[k], recv_sem=prod_recv.at[local],
                device_id=to_core, device_id_type=pl.DeviceIdType.MESH,
            ),
            pltpu.make_async_copy(source, dense_out.at[0, rows_at], out_sem.at[2 + local]),
        )

    def dense_work(k, width):
        at = pl.ds(k * block, width * block)
        query = lax.dot_general(og_all[at, :], b_v[...], NT, preferred_element_type=F32)
        for w in range(width):
            j = origin(k + w)
            q_part[pl.ds(pl.multiple_of(j * block, block), block), :] = jnp.where(
                own_mask(j * block, block), query[w * block:(w + 1) * block], 0.0
            )

        def body(t, carry):
            cols = pl.ds(pl.multiple_of(t * tile, tile), tile)
            prod[at, cols] = lax.dot_general(
                og_all[at, :], w_v[cols, :], NT, preferred_element_type=F32
            )
            return carry

        lax.fori_loop(0, hidden // tile, body, 0)
        for w in range(width):
            side, copy, keep = product_copy(k + w)

            @pl.when(side == core)
            def _():
                keep.start()

            @pl.when(side != core)
            def _():
                copy.start()

    z_part[...] = jnp.zeros_like(z_part)
    a_load.wait()
    forward(1, 0)
    z_work(0, tenants // 2)
    forward(1, 1)
    z_work(tenants // 2, tenants)
    z_copies = scatter(z_part, z_got, z_send, z_recv)
    og_load.wait()
    w_load.wait()
    b_load.wait()
    z_spread = None
    dense_done = 0
    for distance in range(2, half_n):
        forward(distance, 0)
        if distance == 2:
            dense_work(0, 1)
        dense_work(slot(0, distance - 1), 2)
        dense_done = distance - 1
        forward(distance, 1)
        if z_spread is None:
            z_spread = spread(z_part, z_got, z_all, z_copies, z_send, z_recv)
    if z_spread is None:
        dense_work(0, 1)
        z_spread = spread(z_part, z_got, z_all, z_copies, z_send, z_recv)
    for distance in range(dense_done + 1, half_n):
        dense_work(slot(0, distance), 2)
    landed(z_all, z_recv, z_send)
    z_swap = swap(z_all, 2)
    for way in range(2):
        hops[way, half_n, 0].wait_recv()
    at = pl.ds((n - 1) * block, block)
    dense_work(n - 1, 1)

    q_core = pltpu.make_async_remote_copy(
        src_ref=q_part.at[theirs], dst_ref=q_peer,
        send_sem=core_send.at[3], recv_sem=core_recv.at[3],
        device_id=to_core, device_id_type=pl.DeviceIdType.MESH,
    )
    q_core.start()
    swap_landed(z_all, 2)

    def r_work(k):
        j = origin(k)
        here = pl.ds(pl.multiple_of(j * block, block), block)
        r = jnp.where(own_mask(j * block, block), ADAPTER_SCALE * z_all[here, :] * mix[here, :], 0.0)
        high, low = split_bf16(r)
        r_rows[pl.ds(k * block, block), :] = jnp.concatenate([high, low], axis=1)

    for k in range(n):
        r_work(k)
    q_core.wait_recv()
    q_half[...] = q_part[mine, :] + q_peer[...]
    q_copies = scatter(q_half, q_got, q_send, q_recv)

    def grad_b_step(t, carry):
        cols = pl.ds(pl.multiple_of(t * 256, 256), 256)
        both = lax.dot_general(r_rows[...], og_all[:, cols], TN, preferred_element_type=F32)
        grad_b_out[:, cols] = both[:span] + both[span:]
        return carry

    width = og.shape[1] // 256
    lax.fori_loop(0, width, grad_b_step, 0)
    q_spread = spread(q_half, q_got, q_all, q_copies, q_send, q_recv)

    landed(q_all, q_recv, q_send)
    q_swap = swap(q_all, 4)
    for k in range(n):
        side, copy, keep = product_copy(k)

        @pl.when(side == core)
        def _():
            keep.wait()
            copy.wait_recv()

        @pl.when(side != core)
        def _():
            copy.wait_send()

    for copy in hops.values():
        copy.wait_send()
    for copy in z_copies + z_spread + q_copies + q_spread + [z_swap, q_core, q_swap]:
        copy.wait_send()
    for term, (remote, local) in enumerate(hid_copies):
        remote.wait_send()
        local.wait()
        pltpu.make_async_remote_copy(
            src_ref=hid.at[pl.ds(term * rows, rows)], dst_ref=hid_out.at[term, theirs],
            send_sem=core_send.at[term], recv_sem=core_recv.at[term],
            device_id=to_core, device_id_type=pl.DeviceIdType.MESH,
        ).wait_recv()
    swap_landed(q_all, 4)
    q_out[...] = q_all[...]


def tail_kernel(
    tenants_here, counts, side, gate, up, dense, hid, a_in, q_all, mix,
    d_gate, d_up, grad_a, p_rows, p_turned, total, acc,
):
    tokens, span = q_all.shape
    rows, tile = gate.shape
    tenants = a_in.shape[0]
    core = side[0]
    first = core * rows

    @pl.when(pl.program_id(0) == 0)
    def _():
        p = ADAPTER_SCALE * q_all[...] * mix[...]
        turned_high, turned_low = split_bf16(jnp.transpose(p))
        p_turned[:span, :] = turned_high
        p_turned[span:, :] = turned_low
        start = pl.multiple_of(first, rows)
        high, low = split_bf16(
            ADAPTER_SCALE * q_all[pl.ds(start, rows), :] * mix[pl.ds(start, rows), :]
        )
        p_rows[:, :span] = high
        p_rows[:, span:] = low

    total[...] = dense[0] + dense[1]
    starts = [jnp.int32(0)]
    for i in range(tenants):
        starts.append(starts[i] + counts[i])
    for i in range(tenants):
        lower, upper = starts[i], starts[i + 1]

        @pl.when(jnp.logical_and(lower < first + rows, upper > first))
        def _():
            at = lax.broadcasted_iota(jnp.int32, (rows, 2 * span), 0) + first
            inside = jnp.logical_and(at >= lower, at < upper)
            left = jnp.where(inside, p_rows[...].astype(F32), 0.0).astype(BF16)
            factor = a_in[i]
            total[...] += lax.dot_general(
                left, jnp.concatenate([factor, factor], axis=1), NT, preferred_element_type=F32
            )

    height = 16

    def step(i, carry):
        at = pl.ds(pl.multiple_of(i * height, height), height)
        g = gate[at, :].astype(F32)
        u = up[at, :].astype(F32)
        dh = total[at, :]
        sig = jax.nn.sigmoid(g)
        d_up[at, :] = (dh * (g * sig)).astype(BF16)
        d_gate[at, :] = (dh * u * sig * (1.0 + g * (1.0 - sig))).astype(BF16)
        return carry

    lax.fori_loop(0, rows // height, step, 0, unroll=4)

    piece = 256
    for i in range(tenants_here):
        tenant = core * tenants_here + i
        lower = jnp.int32(0)
        for k in range(tenants):
            lower = lower + jnp.where(k < tenant, counts[k], 0)
        upper = lower + counts[tenant]
        acc[...] = jnp.zeros_like(acc)
        for t in range(tokens // piece):
            base = t * piece

            @pl.when(jnp.logical_and(lower < base + piece, upper > base))
            def _():
                at = lax.broadcasted_iota(jnp.int32, (2 * span, piece), 1) + base
                inside = jnp.logical_and(at >= lower, at < upper)
                left = jnp.where(inside, p_turned[:, base:base + piece].astype(F32), 0.0)
                left = left.astype(BF16)
                both = jnp.dot(left, hid[0, base:base + piece, :], preferred_element_type=F32)
                low = jnp.dot(left[:span], hid[1, base:base + piece, :], preferred_element_type=F32)
                acc[...] += both[:span] + both[span:] + low

        grad_a[i] = jnp.transpose(acc[...])


def shards(
    n, output_gradient, gate_preactivation, up_preactivation, frozen_down_weight,
    adapter_input_factor, adapter_output_factor, tenant_token_count, tenant_owner_index,
    token_expert_index, routing_weight_pair,
):
    tokens = token_expert_index.shape[0]
    rows, hidden = gate_preactivation.shape
    tenants, _, span = adapter_input_factor.shape
    block, width = output_gradient.shape
    half_n = n // 2
    part = rows // n
    expert_col = lax.broadcasted_iota(jnp.int32, (1, span), 1) // EXPERT_RANK
    mix = routing_weight_pair[:, 0:1] * (token_expert_index[:, 0:1] == expert_col).astype(F32)
    mix = mix + routing_weight_pair[:, 1:2] * (token_expert_index[:, 1:2] == expert_col).astype(F32)

    any_spec = pl.BlockSpec(memory_space=pl.ANY)
    smem = pl.BlockSpec(memory_space=pltpu.SMEM)
    vmem = pl.BlockSpec(memory_space=pltpu.VMEM)
    dma = pltpu.SemaphoreType.DMA
    dense, hid, q_all, grad_b = pl.pallas_call(
        functools.partial(gather_kernel, n),
        out_shape=(
            jax.ShapeDtypeStruct((2, rows, hidden), F32),
            jax.ShapeDtypeStruct((2, tokens, hidden), BF16),
            jax.ShapeDtypeStruct((tokens, span), F32),
            jax.ShapeDtypeStruct((span, width), F32),
        ),
        in_specs=[smem, smem] + [any_spec] * 6 + [vmem],
        out_specs=(any_spec, any_spec, vmem, vmem),
        scratch_shapes=[
            pltpu.VMEM((tokens, width), BF16),
            pltpu.VMEM((hidden, width), BF16),
            pltpu.VMEM((rows, hidden), BF16),
            pltpu.VMEM((rows, hidden), BF16),
            pltpu.VMEM((tenants, hidden, span), BF16),
            pltpu.VMEM((span, width), BF16),
            pltpu.VMEM((2 * rows, hidden), BF16),
            pltpu.VMEM((tokens, hidden), F32),
            pltpu.VMEM((rows, span), F32),
            pltpu.VMEM((n, part, span), F32),
            pltpu.VMEM((tokens, span), F32),
            pltpu.VMEM((tokens, span), F32),
            pltpu.VMEM((rows, span), F32),
            pltpu.VMEM((rows, span), F32),
            pltpu.VMEM((n, part, span), F32),
            pltpu.VMEM((tokens, span), F32),
            pltpu.VMEM((tokens, 2 * span), BF16),
            dma((6,)),
            dma((2, half_n, 2)),
            dma((2, half_n, 2)),
            dma((n,)),
            dma((half_n,)),
            dma((2, n)),
            dma((2, n)),
            dma((2, n)),
            dma((2, n)),
            dma((5,)),
            dma((5,)),
            dma((2 + half_n,)),
        ],
        compiler_params=pltpu.CompilerParams(
            collective_id=0, has_side_effects=True, vmem_limit_bytes=60 * 1024 * 1024
        ),
        name="gather_products",
    )(
        tenant_token_count, tenant_owner_index, output_gradient, gate_preactivation,
        up_preactivation, frozen_down_weight, adapter_input_factor, adapter_output_factor[0], mix,
    )

    side = lax.axis_index("tensor").astype(jnp.int32)[None]
    tile = 256 if hidden % 256 == 0 else 128
    here = tenants // 2
    wide = pl.BlockSpec((rows, tile), lambda f: (0, f))
    d_gate, d_up, grad_a = pl.pallas_call(
        functools.partial(tail_kernel, here),
        grid=(hidden // tile,),
        out_shape=(
            jax.ShapeDtypeStruct((rows, hidden), BF16),
            jax.ShapeDtypeStruct((rows, hidden), BF16),
            jax.ShapeDtypeStruct((here, hidden, span), F32),
        ),
        in_specs=[
            smem, smem, wide, wide,
            pl.BlockSpec((2, rows, tile), lambda f: (0, 0, f)),
            pl.BlockSpec((2, tokens, tile), lambda f: (0, 0, f)),
            pl.BlockSpec((tenants, tile, span), lambda f: (0, f, 0)),
            pl.BlockSpec((tokens, span), lambda f: (0, 0)),
            pl.BlockSpec((tokens, span), lambda f: (0, 0)),
        ],
        out_specs=(wide, wide, pl.BlockSpec((here, tile, span), lambda f: (0, f, 0))),
        scratch_shapes=[
            pltpu.VMEM((rows, 2 * span), BF16),
            pltpu.VMEM((2 * span, tokens), BF16),
            pltpu.VMEM((rows, tile), F32),
            pltpu.VMEM((span, tile), F32),
        ],
        compiler_params=pltpu.CompilerParams(vmem_limit_bytes=48 * 1024 * 1024),
        name="tail",
    )(
        tenant_token_count, side, gate_preactivation, up_preactivation, dense, hid,
        adapter_input_factor, q_all, mix,
    )
    return d_gate, d_up, grad_a, grad_b[None]


def solution(mesh):
    in_specs = (
        P(("groups", "dp"), "tensor"),
        P(("groups", "tensor"), "dp"),
        P(("groups", "tensor"), "dp"),
        P("dp", "tensor"),
        P("groups", "dp", None),
        P(("groups", "dp"), None, "tensor"),
        P("groups"),
        P("groups"),
        P("groups", None),
        P("groups", None),
    )
    out_specs = (
        P(("groups", "tensor"), "dp"),
        P(("groups", "tensor"), "dp"),
        P(("groups", "tensor"), "dp", None),
        P(("groups", "dp"), None, "tensor"),
    )
    return jax.shard_map(
        functools.partial(shards, mesh.shape["dp"]),
        mesh=mesh, in_specs=in_specs, out_specs=out_specs, check_vma=False,
    )
```

time: 262 us -> 113 us (0.43); the launches traced: 257 us -> 114 us
  waiting for transfers between devices: 131 us -> 0 us
  Pallas kernels: 49.9 us -> 107 us
  other arithmetic: 23.1 us -> 1.52 us
  matrix products: 19 us -> 0 us
  local copies, waits for them, and re-layouts: 19.3 us -> 4.63 us
  between operations: 13.9 us -> 0.69 us
    pallas_call x0 -> x2, Pallas kernels: none -> 107 us  [the longest x1 78.4 us: shards(): pl.pallas_call(functools.partial(gather_kernel, n), out_shape=(jax.ShapeD...]
    psum x1 -> x0, waiting for transfers between devices: 83.3 us -> none  [shards(): q_all = lax.psum(q_part, ('dp', 'tensor'))]
    all_gather x1 -> x0, waiting for transfers between devices: 47.3 us -> none  [shards(): piece = lax.all_gather(output_gradient, 'dp', axis=0, tiled=True)]
    another operation x3 -> x0, Pallas kernels: 46.9 us -> none
    dot_general x2 -> x0, matrix products: 19 us -> none  [the longest x1 13.2 us: shards(): lax.dot_general(piece, stacked_weight, (((1,), (1,)), ((), ())), preferre...]
    transpose x1 -> x0, local copies, waits for them, and re-layouts: 8.54 us -> none  [shards(): input_factor_turned = jnp.swapaxes(input_factor_wide, 1, 2)]
    mul x3 -> x0, other arithmetic: 7.67 us -> none  [the longest x1 4.99 us: shards(): hidden_state = silu * up]
    transpose x1 -> x0, other arithmetic: 6.82 us -> none  [shards(): input_factor_turned = jnp.swapaxes(input_factor_wide, 1, 2)]
  transfers between devices with their start and end apart: 4 -> 0, of which waited for: 2 -> 0; matrix products, arithmetic and copies ran while one was open for 17% -> 0% of each run, Pallas kernels for 19% -> 0%
where the time goes in v1:
time: 113 us; the launch traced here: 114 us
  Pallas kernels  107 us (95%)
  local copies, waits for them, and re-layouts  4.63 us (4%)
  other arithmetic  1.52 us (1%)
    pallas_call x1, Pallas kernels, shards(): pl.pallas_call(functools.partial(gather_kernel, n), out_shape=(jax.ShapeD...  78.4 us
    pallas_call x1, Pallas kernels, shards(): pl.pallas_call(functools.partial(tail_kernel, here), grid=(hidden // tile...  28.3 us
    unnamed x13, local copies, waits for them, and re-layouts  3.06 us

profile of v1, /device:TPU:1, one launch (start us, length us, event | category | flops | bytes accessed | tf_op | source)
XLA Modules:
  0.0 113.5 jit_solution(8060413083386964770)
XLA Ops:
  0.6 0.8 fusion
  1.4 0.8 fusion.1
  2.2 1.5 %select_add_fusion.mix = f32[1024,128]{1,0:T(8,128)} fusion(f32[1024]{0:T(1024)S(1)} %bitcast.12, f32[1024]{0:T(1024)S(1)} %bitcast.11, s32[128]{0:T(128)S(1)} %and_select_fusion, s32[1024]{0:T(1024)S(1)} %bitcast.10, s32[1024]{0:T(1024)S(1)} %bitcast.9), kind=kLoop, calls=%fused_computation | loop fusion | flops 655360 | bytes 541184 | tf_op jit(solution)/shard_map/add | solution.py:472
  3.7 0.0 copy-start
  3.7 0.0 copy-start.1
  3.7 0.0 copy-start.4
  3.7 78.4 %gather_products.1 = (f32[2,512,1792]{2,1,0:T(8,128)}, bf16[2,1024,1792]{2,1,0:T(8,128)(2,1)}, f32[1024,128]{1,0:T(8,128)}, f32[128,2048]{1,0:T(8,128)}) custom-call(s32[8]{0:T(128)} %counts.3, s32[8]{0:T(128)} %owners.1, bf16[128,2048]{1,0:T(8,128)(2,1)} %og.1, bf16[512,1792]{1,0:T(8,128)(2,1)} %gate.3, bf16[512,1792]{1,0:T(8,128)(2,1)} %up.3, ...), custom_call_target="tpu_custom_call" | custom-call | tf_op jit(solution)/shard_map/gather_products/pallas_call | solution.py:478
  82.2 0.0 copy-done
  82.2 0.0 copy-done.1
  82.2 0.0 copy-done.4
  82.2 0.0 copy-start.2
  82.2 1.0 copy-done.2
  83.3 0.0 copy-start.3
  83.3 1.0 copy-done.3
  84.3 0.0 copy-start.5
  84.3 28.3 %tail.1 = (bf16[512,1792]{1,0:T(8,128)(2,1)}, bf16[512,1792]{1,0:T(8,128)(2,1)}, f32[4,1792,128]{2,1,0:T(8,128)}) custom-call(s32[8]{0:T(128)S(1)} %copy-done.4, s32[1]{0:T(128)} %bitcast.side, bf16[512,1792]{1,0:T(8,128)(2,1)S(1)} %copy-done, bf16[512,1792]{1,0:T(8,128)(2,1)S(1)} %copy-done.1, f32[2,512,1792]{2,1,0:T(8,128)} %get-tuple-element.11.dense, ...), custom_call_target="tpu_custom_call" | custom-call | tf_op jit(solution)/shard_map/tail/pallas_call | solution.py:532
  112.6 0.0 copy-done.5
  112.6 1.0 copy.15
  (1 shorter events, 0.0 us)
Async XLA Ops:
  3.7 78.5 %copy-start = (bf16[512,1792]{1,0:T(8,128)(2,1)S(1)}, bf16[512,1792]{1,0:T(8,128)(2,1)}, u32[]{:S(2)}) copy-start(bf16[512,1792]{1,0:T(8,128)(2,1)} %gate.3) | copy-start | bytes 5505028
  3.7 78.5 %copy-start.1 = (bf16[512,1792]{1,0:T(8,128)(2,1)S(1)}, bf16[512,1792]{1,0:T(8,128)(2,1)}, u32[]{:S(2)}) copy-start(bf16[512,1792]{1,0:T(8,128)(2,1)} %up.3) | copy-start | bytes 5505028
  3.7 78.5 %copy-start.4 = (s32[8]{0:T(128)S(1)}, s32[8]{0:T(128)}, u32[]{:S(2)}) copy-start(s32[8]{0:T(128)} %counts.3) | copy-start | bytes 100
  82.2 1.0 copy-start.2
  83.3 1.0 copy-start.3
  84.3 28.3 %copy-start.5 = (f32[128,2048]{1,0:T(8,128)S(1)}, f32[128,2048]{1,0:T(8,128)}, u32[]{:S(2)}) copy-start(f32[128,2048]{1,0:T(8,128)} %get-tuple-element.17) | copy-start | bytes 3145732

commit v2 on v1

--- a/solution.py
+++ b/solution.py
@@ -137,7 +137,7 @@
         hid[low_at, :] = low
         return carry
 
-    lax.fori_loop(0, rows // height, hidden_step, 0)
+    lax.fori_loop(0, rows // height, hidden_step, 0, unroll=2)
 
     to_core = {"tensor": other}
     mine = pl.ds(core * rows, rows)
@@ -256,7 +256,7 @@
             pltpu.make_async_copy(source, dense_out.at[0, rows_at], out_sem.at[2 + local]),
         )
 
-    def dense_work(k, width):
+    def query_work(k, width):
         at = pl.ds(k * block, width * block)
         query = lax.dot_general(og_all[at, :], b_v[...], NT, preferred_element_type=F32)
         for w in range(width):
@@ -264,6 +264,11 @@
             q_part[pl.ds(pl.multiple_of(j * block, block), block), :] = jnp.where(
                 own_mask(j * block, block), query[w * block:(w + 1) * block], 0.0
             )
+
+    def dense_work(k, width):
+        if k < n - 1:
+            query_work(k, width)
+        at = pl.ds(k * block, width * block)
 
         def body(t, carry):
             cols = pl.ds(pl.multiple_of(t * tile, tile), tile)
@@ -314,8 +319,7 @@
     z_swap = swap(z_all, 2)
     for way in range(2):
         hops[way, half_n, 0].wait_recv()
-    at = pl.ds((n - 1) * block, block)
-    dense_work(n - 1, 1)
+    query_work(n - 1, 1)
 
     q_core = pltpu.make_async_remote_copy(
         src_ref=q_part.at[theirs], dst_ref=q_peer,
@@ -337,6 +341,7 @@
     q_core.wait_recv()
     q_half[...] = q_part[mine, :] + q_peer[...]
     q_copies = scatter(q_half, q_got, q_send, q_recv)
+    dense_work(n - 1, 1)
 
     def grad_b_step(t, carry):
         cols = pl.ds(pl.multiple_of(t * 256, 256), 256)
@@ -344,10 +349,8 @@
         grad_b_out[:, cols] = both[:span] + both[span:]
         return carry
 
-    width = og.shape[1] // 256
-    lax.fori_loop(0, width, grad_b_step, 0)
     q_spread = spread(q_half, q_got, q_all, q_copies, q_send, q_recv)
-
+    lax.fori_loop(0, og.shape[1] // 256, grad_b_step, 0)
     landed(q_all, q_recv, q_send)
     q_swap = swap(q_all, 4)
     for k in range(n):
@@ -388,43 +391,46 @@
     core = side[0]
     first = core * rows
 
+    starts = [jnp.int32(0)]
+    for i in range(tenants):
+        starts.append(starts[i] + counts[i])
+    bounds = []
+    for i in range(tenants_here):
+        upper_half = core == 1
+        bounds.append((
+            jnp.where(upper_half, starts[tenants_here + i], starts[i]),
+            jnp.where(upper_half, starts[tenants_here + i + 1], starts[i + 1]),
+        ))
+
     @pl.when(pl.program_id(0) == 0)
     def _():
         p = ADAPTER_SCALE * q_all[...] * mix[...]
-        turned_high, turned_low = split_bf16(jnp.transpose(p))
-        p_turned[:span, :] = turned_high
-        p_turned[span:, :] = turned_low
+        turned = jnp.transpose(p)
+        at = lax.broadcasted_iota(jnp.int32, (span, tokens), 1)
+        for i in range(tenants_here):
+            inside = jnp.logical_and(at >= bounds[i][0], at < bounds[i][1])
+            high, low = split_bf16(jnp.where(inside, turned, 0.0))
+            p_turned[i, :span, :] = high
+            p_turned[i, span:, :] = low
         start = pl.multiple_of(first, rows)
-        high, low = split_bf16(
-            ADAPTER_SCALE * q_all[pl.ds(start, rows), :] * mix[pl.ds(start, rows), :]
-        )
-        p_rows[:, :span] = high
-        p_rows[:, span:] = low
-
-    total[...] = dense[0] + dense[1]
-    starts = [jnp.int32(0)]
-    for i in range(tenants):
-        starts.append(starts[i] + counts[i])
-    for i in range(tenants):
-        lower, upper = starts[i], starts[i + 1]
-
-        @pl.when(jnp.logical_and(lower < first + rows, upper > first))
-        def _():
-            at = lax.broadcasted_iota(jnp.int32, (rows, 2 * span), 0) + first
-            inside = jnp.logical_and(at >= lower, at < upper)
-            left = jnp.where(inside, p_rows[...].astype(F32), 0.0).astype(BF16)
-            factor = a_in[i]
-            total[...] += lax.dot_general(
-                left, jnp.concatenate([factor, factor], axis=1), NT, preferred_element_type=F32
-            )
-
-    height = 16
+        own = ADAPTER_SCALE * q_all[pl.ds(start, rows), :] * mix[pl.ds(start, rows), :]
+        at = lax.broadcasted_iota(jnp.int32, (rows, span), 0) + first
+        for i in range(tenants):
+            inside = jnp.logical_and(at >= starts[i], at < starts[i + 1])
+            high, low = split_bf16(jnp.where(inside, own, 0.0))
+            p_rows[:, 2 * i * span:(2 * i + 1) * span] = high
+            p_rows[:, (2 * i + 1) * span:(2 * i + 2) * span] = low
+
+    factors = jnp.concatenate([a_in[i // 2] for i in range(2 * tenants)], axis=1)
+    total[...] = lax.dot_general(p_rows[...], factors, NT, preferred_element_type=F32)
+
+    height = 32
 
     def step(i, carry):
         at = pl.ds(pl.multiple_of(i * height, height), height)
         g = gate[at, :].astype(F32)
         u = up[at, :].astype(F32)
-        dh = total[at, :]
+        dh = total[at, :] + (dense[0, at, :] + dense[1, at, :])
         sig = jax.nn.sigmoid(g)
         d_up[at, :] = (dh * (g * sig)).astype(BF16)
         d_gate[at, :] = (dh * u * sig * (1.0 + g * (1.0 - sig))).astype(BF16)
@@ -432,23 +438,16 @@
 
     lax.fori_loop(0, rows // height, step, 0, unroll=4)
 
-    piece = 256
+    piece = 512
     for i in range(tenants_here):
-        tenant = core * tenants_here + i
-        lower = jnp.int32(0)
-        for k in range(tenants):
-            lower = lower + jnp.where(k < tenant, counts[k], 0)
-        upper = lower + counts[tenant]
+        lower, upper = bounds[i]
         acc[...] = jnp.zeros_like(acc)
         for t in range(tokens // piece):
             base = t * piece
 
             @pl.when(jnp.logical_and(lower < base + piece, upper > base))
             def _():
-                at = lax.broadcasted_iota(jnp.int32, (2 * span, piece), 1) + base
-                inside = jnp.logical_and(at >= lower, at < upper)
-                left = jnp.where(inside, p_turned[:, base:base + piece].astype(F32), 0.0)
-                left = left.astype(BF16)
+                left = p_turned[i, :, base:base + piece]
                 both = jnp.dot(left, hid[0, base:base + piece, :], preferred_element_type=F32)
                 low = jnp.dot(left[:span], hid[1, base:base + piece, :], preferred_element_type=F32)
                 acc[...] += both[:span] + both[span:] + low
@@ -547,8 +546,8 @@
         ],
         out_specs=(wide, wide, pl.BlockSpec((here, tile, span), lambda f: (0, f, 0))),
         scratch_shapes=[
-            pltpu.VMEM((rows, 2 * span), BF16),
-            pltpu.VMEM((2 * span, tokens), BF16),
+            pltpu.VMEM((rows, 2 * tenants * span), BF16),
+            pltpu.VMEM((here, 2 * span, tokens), BF16),
             pltpu.VMEM((rows, tile), F32),
             pltpu.VMEM((span, tile), F32),
         ],

time: 113 us -> 107 us (0.947)
  Pallas kernels: 107 us -> 99.8 us
    pallas_call x1, Pallas kernels: 28.3 us -> 24.3 us  [shards(): pl.pallas_call(functools.partial(tail_kernel, here), grid=(hidden // tile...]
    pallas_call x1, Pallas kernels: 78.4 us -> 75.5 us  [shards(): pl.pallas_call(functools.partial(gather_kernel, n), out_shape=(jax.ShapeD...]
where the time goes in v2:
time: 107 us
  Pallas kernels  99.8 us (93%)
  local copies, waits for them, and re-layouts  4.63 us (4%)
  other arithmetic  1.52 us (1%)
    pallas_call x1, Pallas kernels, shards(): pl.pallas_call(functools.partial(gather_kernel, n), out_shape=(jax.ShapeD...  75.5 us
    pallas_call x1, Pallas kernels, shards(): pl.pallas_call(functools.partial(tail_kernel, here), grid=(hidden // tile...  24.3 us
    unnamed x13, local copies, waits for them, and re-layouts  3.06 us

profile of v2, /device:TPU:1, one launch (start us, length us, event | category | flops | bytes accessed | tf_op | source)
XLA Modules:
  0.0 106.6 jit_solution(12767587467410430120)
XLA Ops:
  0.6 0.8 fusion
  1.4 0.8 fusion.1
  2.2 1.5 %select_add_fusion.mix = f32[1024,128]{1,0:T(8,128)} fusion(f32[1024]{0:T(1024)S(1)} %bitcast.12, f32[1024]{0:T(1024)S(1)} %bitcast.11, s32[128]{0:T(128)S(1)} %and_select_fusion, s32[1024]{0:T(1024)S(1)} %bitcast.10, s32[1024]{0:T(1024)S(1)} %bitcast.9), kind=kLoop, calls=%fused_computation | loop fusion | flops 655360 | bytes 541184 | tf_op jit(solution)/shard_map/add | solution.py:471
  3.7 0.0 copy-start
  3.7 0.0 copy-start.1
  3.7 0.0 copy-start.4
  3.7 75.5 %gather_products.1 = (f32[2,512,1792]{2,1,0:T(8,128)}, bf16[2,1024,1792]{2,1,0:T(8,128)(2,1)}, f32[1024,128]{1,0:T(8,128)}, f32[128,2048]{1,0:T(8,128)}) custom-call(s32[8]{0:T(128)} %counts.3, s32[8]{0:T(128)} %owners.1, bf16[128,2048]{1,0:T(8,128)(2,1)} %og.1, bf16[512,1792]{1,0:T(8,128)(2,1)} %gate.3, bf16[512,1792]{1,0:T(8,128)(2,1)} %up.3, ...), custom_call_target="tpu_custom_call" | custom-call | tf_op jit(solution)/shard_map/gather_products/pallas_call | solution.py:477
  79.2 0.0 copy-done
  79.2 0.0 copy-done.1
  79.2 0.0 copy-done.4
  79.2 0.0 copy-start.2
  79.3 1.0 copy-done.2
  80.3 0.0 copy-start.3
  80.3 1.0 copy-done.3
  81.3 0.0 copy-start.5
  81.3 24.3 %tail.1 = (bf16[512,1792]{1,0:T(8,128)(2,1)}, bf16[512,1792]{1,0:T(8,128)(2,1)}, f32[4,1792,128]{2,1,0:T(8,128)}) custom-call(s32[8]{0:T(128)S(1)} %copy-done.4, s32[1]{0:T(128)} %bitcast.side, bf16[512,1792]{1,0:T(8,128)(2,1)S(1)} %copy-done, bf16[512,1792]{1,0:T(8,128)(2,1)S(1)} %copy-done.1, f32[2,512,1792]{2,1,0:T(8,128)} %get-tuple-element.11.dense, ...), custom_call_target="tpu_custom_call" | custom-call | tf_op jit(solution)/shard_map/tail/pallas_call | solution.py:531
  105.6 0.0 copy-done.5
  105.7 1.0 copy.15
  (1 shorter events, 0.0 us)
Async XLA Ops:
  3.7 75.5 %copy-start = (bf16[512,1792]{1,0:T(8,128)(2,1)S(1)}, bf16[512,1792]{1,0:T(8,128)(2,1)}, u32[]{:S(2)}) copy-start(bf16[512,1792]{1,0:T(8,128)(2,1)} %gate.3) | copy-start | bytes 5505028
  3.7 75.5 %copy-start.1 = (bf16[512,1792]{1,0:T(8,128)(2,1)S(1)}, bf16[512,1792]{1,0:T(8,128)(2,1)}, u32[]{:S(2)}) copy-start(bf16[512,1792]{1,0:T(8,128)(2,1)} %up.3) | copy-start | bytes 5505028
  3.7 75.5 %copy-start.4 = (s32[8]{0:T(128)S(1)}, s32[8]{0:T(128)}, u32[]{:S(2)}) copy-start(s32[8]{0:T(128)} %counts.3) | copy-start | bytes 100
  79.2 1.0 copy-start.2
  80.3 1.0 copy-start.3
  81.3 24.3 %copy-start.5 = (f32[128,2048]{1,0:T(8,128)S(1)}, f32[128,2048]{1,0:T(8,128)}, u32[]{:S(2)}) copy-start(f32[128,2048]{1,0:T(8,128)} %get-tuple-element.17) | copy-start | bytes 3145732
